TPU v7x, 32 devices: a whole 2x2x4 slice. The times are simulated.
32 devices in a mesh: seq: 4 (over z), chan: 4 (over y, x), dp: 2 (over core).
Axes of the slice: x: 2, y: 2, z: 4, core: 2. Of those that a mesh axis runs over, the one named last changes fastest.
Arguments:
- query_proj: bfloat16 [2, 2048, 8192], P('dp', 'seq', 'chan'), may hold values from -6 to 6
- key_proj: bfloat16 [2, 2048, 8192], P('dp', 'seq', 'chan')
- value_proj: bfloat16 [2, 2048, 8192], P('dp', 'seq', 'chan')
- cotangent: bfloat16 [2, 2048, 8192], P('dp', 'seq', 'chan'), may hold values from -6 to 6
- long_filter: float32 [2048, 8192], P('seq', 'chan')
- skip_gain: float32 [8192], P('chan'), may hold values from -3 to 3
Outputs:
- output: bfloat16 [2, 2048, 8192], P('dp', 'seq', 'chan')
- grad_query: bfloat16 [2, 2048, 8192], P('dp', 'seq', 'chan')
- grad_key: bfloat16 [2, 2048, 8192], P('dp', 'seq', 'chan')
- grad_value: bfloat16 [2, 2048, 8192], P('dp', 'seq', 'chan')
- grad_filter: float32 [2048, 8192], P('seq', 'chan')
- grad_skip: float32 [8192], P('chan')
All inputs are finite; a program needn't handle non-finite values.
Results may differ from a plain program's by a relative error of at most 0.0095.
Values may be sent and summed in bfloat16 or wider, within the bound.
A program may use at most 128 MiB of HBM per device.

v0:
```python
import math

import jax
import jax.numpy as jnp
from jax import lax
from jax.sharding import PartitionSpec as P

full_precision = lax.Precision.HIGHEST


def dft_tables(seq_length):
    full_size = 2 * seq_length
    inner_size = 128
    outer_size = full_size // inner_size
    half_size = outer_size // 2
    outer_index = jnp.arange(outer_size, dtype=jnp.int32)
    half_index = jnp.arange(half_size, dtype=jnp.int32)
    inner_index = jnp.arange(inner_size, dtype=jnp.int32)
    first_angle = (
        2.0
        * math.pi
        / outer_size
        * (outer_index[:, None] * half_index[None, :] % outer_size).astype(jnp.float32)
    )
    twist_angle = (
        2.0
        * math.pi
        / full_size
        * (outer_index[:, None] * inner_index[None, :] % full_size).astype(jnp.float32)
    )
    last_angle = (
        2.0
        * math.pi
        / inner_size
        * (inner_index[:, None] * inner_index[None, :] % inner_size).astype(jnp.float32)
    )
    return (
        jnp.cos(first_angle),
        jnp.sin(first_angle),
        jnp.cos(twist_angle),
        jnp.sin(twist_angle),
        jnp.cos(last_angle),
        jnp.sin(last_angle),
    )


def forward(signal, tables):
    cos_first, sin_first, cos_twist, sin_twist, cos_last, sin_last = tables
    half_size = cos_first.shape[1]
    signal_grid = signal.reshape(signal.shape[0], half_size, 128)
    real_first = jnp.einsum("kn,rnm->rkm", cos_first, signal_grid, precision=full_precision)
    imag_first = -jnp.einsum("kn,rnm->rkm", sin_first, signal_grid, precision=full_precision)
    real_twist = real_first * cos_twist + imag_first * sin_twist
    imag_twist = imag_first * cos_twist - real_first * sin_twist
    real_last = jnp.einsum(
        "rkm,mj->rkj", real_twist, cos_last, precision=full_precision
    ) + jnp.einsum("rkm,mj->rkj", imag_twist, sin_last, precision=full_precision)
    imag_last = jnp.einsum(
        "rkm,mj->rkj", imag_twist, cos_last, precision=full_precision
    ) - jnp.einsum("rkm,mj->rkj", real_twist, sin_last, precision=full_precision)
    return (real_last, imag_last)


def inverse(real_part, imag_part, tables):
    cos_first, sin_first, cos_twist, sin_twist, cos_last, sin_last = tables
    half_size = cos_first.shape[1]
    row_total = real_part.shape[0]
    real_inner = jnp.einsum(
        "rkj,jm->rkm", real_part, cos_last, precision=full_precision
    ) - jnp.einsum("rkj,jm->rkm", imag_part, sin_last, precision=full_precision)
    imag_inner = jnp.einsum(
        "rkj,jm->rkm", imag_part, cos_last, precision=full_precision
    ) + jnp.einsum("rkj,jm->rkm", real_part, sin_last, precision=full_precision)
    real_twist = real_inner * cos_twist - imag_inner * sin_twist
    imag_twist = imag_inner * cos_twist + real_inner * sin_twist
    result = jnp.einsum(
        "kn,rkm->rnm", cos_first, real_twist, precision=full_precision
    ) - jnp.einsum("kn,rkm->rnm", sin_first, imag_twist, precision=full_precision)
    return (result / (2.0 * half_size * 128)).reshape(row_total, half_size * 128)


def filter_block(items, tables):
    mixed_blk, weighted_blk, kernel = items
    batches, chan_width, seq_length = mixed_blk.shape
    row_count = batches * chan_width
    mixed_wide = mixed_blk.astype(jnp.float32)
    weighted_wide = weighted_blk.astype(jnp.float32)
    stacked = jnp.concatenate(
        [
            mixed_wide.reshape(row_count, seq_length),
            weighted_wide.reshape(row_count, seq_length),
            kernel,
        ],
        axis=0,
    )
    real_spec, imag_spec = forward(stacked, tables)
    grid_shape = real_spec.shape[1:]
    mixed_real = real_spec[:row_count].reshape((batches, chan_width) + grid_shape)
    mixed_imag = imag_spec[:row_count].reshape((batches, chan_width) + grid_shape)
    weighted_real = real_spec[row_count : 2 * row_count].reshape((batches, chan_width) + grid_shape)
    weighted_imag = imag_spec[row_count : 2 * row_count].reshape((batches, chan_width) + grid_shape)
    kernel_real = real_spec[2 * row_count :][None]
    kernel_imag = imag_spec[2 * row_count :][None]
    conv_real = mixed_real * kernel_real - mixed_imag * kernel_imag
    conv_imag = mixed_real * kernel_imag + mixed_imag * kernel_real
    corr_real = kernel_real * weighted_real + kernel_imag * weighted_imag
    corr_imag = kernel_real * weighted_imag - kernel_imag * weighted_real
    slope_real = jnp.sum(mixed_real * weighted_real + mixed_imag * weighted_imag, axis=0)
    slope_imag = jnp.sum(mixed_real * weighted_imag - mixed_imag * weighted_real, axis=0)
    spec_real = jnp.concatenate(
        [
            conv_real.reshape((row_count,) + grid_shape),
            corr_real.reshape((row_count,) + grid_shape),
            slope_real,
        ],
        axis=0,
    )
    spec_imag = jnp.concatenate(
        [
            conv_imag.reshape((row_count,) + grid_shape),
            corr_imag.reshape((row_count,) + grid_shape),
            slope_imag,
        ],
        axis=0,
    )
    result = inverse(spec_real, spec_imag, tables)
    conv_vals = result[:row_count].reshape(batches, chan_width, seq_length).astype(jnp.bfloat16)
    corr_vals = (
        result[row_count : 2 * row_count]
        .reshape(batches, chan_width, seq_length)
        .astype(jnp.bfloat16)
    )
    slope = result[2 * row_count :]
    return (conv_vals, corr_vals, slope)


def run_blocks(mixed_rows, weighted_rows, filter_part):
    batches, part_width, seq_length = mixed_rows.shape
    block_width = min(part_width, 8)
    block_count = part_width // block_width
    tables = dft_tables(seq_length)

    def stack_rows(arr):
        return jnp.moveaxis(arr.reshape(batches, block_count, block_width, seq_length), 1, 0)

    def unstack_rows(arr):
        return jnp.moveaxis(arr, 0, 1).reshape(batches, part_width, seq_length)

    def one_block(items):
        return filter_block(items, tables)

    items = (
        stack_rows(mixed_rows),
        stack_rows(weighted_rows),
        filter_part.reshape(block_count, block_width, seq_length),
    )
    conv_vals, corr_vals, slope = lax.map(one_block, items)
    return (unstack_rows(conv_vals), unstack_rows(corr_vals), slope.reshape(part_width, seq_length))


def on_device(query_proj, key_proj, value_proj, cotangent, long_filter, skip_gain):
    query_rows = query_proj[0].astype(jnp.float32)
    key_rows = key_proj[0].astype(jnp.float32)
    value_rows = value_proj[0].astype(jnp.float32)
    cot_rows = cotangent[0].astype(jnp.float32)
    local_length = query_proj.shape[1]
    chan_width = query_proj.shape[2]
    seq_count = lax.axis_size("seq")
    batch_count = lax.axis_size("dp")
    factor = (batch_count * seq_count * local_length) ** (-0.5)
    mixed = (key_rows * value_rows).astype(jnp.bfloat16)
    weighted = (cot_rows * query_rows).astype(jnp.bfloat16)
    mixed_wide = mixed.astype(jnp.float32)
    weighted_wide = weighted.astype(jnp.float32)
    gain_term = factor * jnp.sum(weighted_wide * mixed_wide, axis=0)
    grad_skip = lax.psum(gain_term, ("seq", "dp"))
    filter_share = lax.all_to_all(long_filter.T, "seq", split_axis=0, concat_axis=1, tiled=True)
    groups = seq_count * batch_count
    share_width = chan_width // groups
    mixed_cols, weighted_cols = (
        lax.all_to_all(mixed.T, ("seq", "dp"), split_axis=0, concat_axis=1, tiled=True),
        lax.all_to_all(weighted.T, ("seq", "dp"), split_axis=0, concat_axis=1, tiled=True),
    )

    def to_sequences(arr):
        arr = arr.reshape(share_width, seq_count, batch_count, local_length)
        return jnp.transpose(arr, (2, 0, 1, 3)).reshape(
            batch_count, share_width, seq_count * local_length
        )

    def to_pieces(arr):
        arr = arr.reshape(batch_count, share_width, seq_count, local_length)
        return jnp.transpose(arr, (1, 2, 0, 3)).reshape(share_width, groups * local_length)

    filter_part = lax.dynamic_slice_in_dim(
        filter_share, lax.axis_index("dp") * share_width, share_width, 0
    )
    conv_vals, corr_vals, slope = run_blocks(
        to_sequences(mixed_cols), to_sequences(weighted_cols), filter_part
    )
    conv_back, corr_back = (
        lax.all_to_all(
            to_pieces(conv_vals), ("seq", "dp"), split_axis=1, concat_axis=0, tiled=True
        ),
        lax.all_to_all(
            to_pieces(corr_vals), ("seq", "dp"), split_axis=1, concat_axis=0, tiled=True
        ),
    )
    slope_share = lax.all_gather(slope, "dp", axis=0, tiled=True)
    slope_rows = lax.all_to_all(slope_share, "seq", split_axis=1, concat_axis=0, tiled=True)
    grad_filter = factor * slope_rows.T
    conv_rows = conv_back.T.astype(jnp.float32)
    corr_rows = corr_back.T.astype(jnp.float32)
    signal = conv_rows + skip_gain[None, :] * mixed_wide
    output = (query_rows * signal).astype(jnp.bfloat16)
    grad_query = (cot_rows * signal).astype(jnp.bfloat16)
    back = corr_rows + skip_gain[None, :] * weighted_wide
    grad_key = (back * value_rows).astype(jnp.bfloat16)
    grad_value = (back * key_rows).astype(jnp.bfloat16)
    return (
        output[None],
        grad_query[None],
        grad_key[None],
        grad_value[None],
        grad_filter,
        grad_skip,
    )


def solution(mesh):
    return jax.shard_map(
        on_device,
        mesh=mesh,
        in_specs=(
            P("dp", "seq", "chan"),
            P("dp", "seq", "chan"),
            P("dp", "seq", "chan"),
            P("dp", "seq", "chan"),
            P("seq", "chan"),
            P("chan"),
        ),
        out_specs=(
            P("dp", "seq", "chan"),
            P("dp", "seq", "chan"),
            P("dp", "seq", "chan"),
            P("dp", "seq", "chan"),
            P("seq", "chan"),
            P("chan"),
        ),
        check_vma=False,
    )
```

profile of v0, /device:TPU:1, one launch (start us, length us, event | category | flops | bytes accessed | tf_op | source)
XLA Modules:
  0.0 958.2 jit_solution(4508333251613805329)
XLA Ops:
  7.2 6.9 fusion.136
  14.1 2.6 copy.53
  16.7 6.5 all-to-all-start.1
  23.2 2.5 copy.51
  25.7 45.8 %all-to-all-done.1 = bf16[8,256,512]{2,1,0:T(8,128)(2,1)} async-done(((bf16[8,256,512]{2,1,0:T(8,128)(2,1)}), bf16[8,256,512]{2,1,0:T(8,128)(2,1)}, u32[]{:S(2)}, u32[]{:S(2)}) %all-to-all-start.1) | async-done | bytes 2097184 | tf_op jit(solution)/shard_map/all_to_all | solution.py:182
  71.5 4.4 all-to-all-start
  75.9 5.3 copy.55
  81.3 5.3 copy.56
  86.5 37.6 %all-to-all-done = bf16[8,256,512]{2,1,0:T(8,128)(2,1)S(1)} async-done(((bf16[8,256,512]{2,1,0:T(8,128)(2,1)}), bf16[8,256,512]{2,1,0:T(8,128)(2,1)S(1)}, u32[]{:S(2)}, u32[]{:S(2)}) %all-to-all-start) | async-done | bytes 2097184 | tf_op jit(solution)/shard_map/all_to_all | solution.py:181
  124.1 4.8 all-to-all-start.2
  129.0 4.5 copy.54
  133.6 4.5 reshape_reshape.13
  138.1 3.0 copy.52
  141.0 4.4 reshape_reshape.12
  145.5 76.2 %all-to-all-done.2 = f32[4,512,512]{1,2,0:T(8,128)} async-done(((f32[4,512,512]{1,2,0:T(8,128)}), f32[4,512,512]{1,2,0:T(8,128)}, u32[]{:S(2)}, u32[]{:S(2)}) %all-to-all-start.2) | async-done | bytes 4194336 | tf_op jit(solution)/shard_map/all_to_all | solution.py:177
  221.7 1.7 constant_dynamic-slice_fusion
  223.4 1.8 copy.57
  225.3 465.4 %while.16 = (s32[]{:T(128)}, bf16[32,2,8,2048]{3,2,1,0:T(8,128)(2,1)}, bf16[32,2,8,2048]{3,2,1,0:T(8,128)(2,1)}, f32[32,8,2048]{2,1,0:T(8,128)}, bf16[32,2,8,204...) while((s32[]{:T(128)}, ...), condition=%wide.region_3.4_spmd.clone.clone, body=%wide.region_0.3_spmd.clone.clone.sunk | while | flops 2147651584 | bytes 28771948 | solution.py:157
  229.7 0.9 convolution_add_fusion.4
  244.3 0.9 convolution_add_fusion.4
  258.8 0.9 convolution_add_fusion.4
  273.4 0.9 convolution_add_fusion.4
  287.9 0.9 convolution_add_fusion.4
  317.0 0.9 convolution_add_fusion.4
  331.5 0.9 convolution_add_fusion.4
  346.1 0.9 convolution_add_fusion.4
  360.6 0.9 convolution_add_fusion.4
  690.7 1.7 copy.60
  692.4 2.8 reshape_reshape.14
  695.1 3.3 copy.61
  698.5 5.0 all-to-all-start.3
  704.2 3.2 copy.63
  707.3 4.5 reshape_reshape.15
  711.8 3.3 copy.64
  715.1 36.5 %all-to-all-done.3 = bf16[256,8,512]{2,0,1:T(8,128)(2,1)S(1)} async-done(((bf16[256,8,512]{2,0,1:T(8,128)(2,1)}), bf16[256,8,512]{2,0,1:T(8,128)(2,1)S(1)}, u32[]{:S(2)}, u32[]{:S(2)}) %all-to-all-start.3) | async-done | bytes 2097184 | tf_op jit(solution)/shard_map/all_to_all | solution.py:202
  751.7 5.1 all-to-all-start.4
  756.8 5.4 copy.66
  762.1 43.0 %all-to-all-done.4 = bf16[256,8,512]{2,0,1:T(8,128)(2,1)} async-done(((bf16[256,8,512]{2,0,1:T(8,128)(2,1)}), bf16[256,8,512]{2,0,1:T(8,128)(2,1)}, u32[]{:S(2)}, u32[]{:S(2)}) %all-to-all-start.4) | async-done | bytes 2097184 | tf_op jit(solution)/shard_map/all_to_all | solution.py:205
  805.1 4.8 all-to-all-start.5
  809.9 97.9 %psum.7 = f32[2048]{0:T(1024)} all-reduce(f32[2048]{0:T(1024)S(1)} %broadcast_multiply_fusion), channel_id=1, replica_groups=mesh['seq'=4,'chan'=4,'dp'=2] {'seq','dp'}, use_global_device_ids=true, to_apply=%region_5.6 | all-reduce | flops 2048 | bytes 16384 | tf_op jit(solution)/shard_map/psum | solution.py:176
  907.9 2.6 convert_element_type.196
  910.5 5.4 copy.62
  915.9 4.2 convert_element_type.197
  920.1 5.6 copy.65
  925.6 10.5 %fusion.143 = (bf16[1,512,2048]{2,1,0:T(8,128)(2,1)}, bf16[1,512,2048]{2,1,0:T(8,128)(2,1)}, bf16[1,512,2048]{2,1,0:T(8,128)(2,1)}, bf16[1,512,2048]{2,1,0:T(8,128)(2,1)}) fusion(bf16[512,2048]{1,0:T(8,128)(2,1)S(1)} %copy-done.1, f32[2048,512]{0,1:T(8,128)} %copy.65, bf16[1,512,2048]{2,1,0:T(8,128)(2,1)} %param.9, f32[2048]{0:T(1024)S(1)} %copy-done.3, ...), kind=kLoop, calls=%fused_computation.174 | loop fusion | flops 18874368 | bytes 29368320 | tf_op jit(solution)/shard_map/broadcast_in_dim | solution.py:224
  936.1 4.7 multiply_bitcast_fusion
  940.8 5.3 copy.67
  946.1 5.3 copy.68
  (1063 shorter events, 451.6 us)
Async XLA Ops:
  14.1 2.6 copy-start
  16.7 6.5 copy-start.2
  16.7 54.8 %all-to-all-start.1 = ((bf16[8,256,512]{2,1,0:T(8,128)(2,1)}), bf16[8,256,512]{2,1,0:T(8,128)(2,1)}, u32[]{:S(2)}, u32[]{:S(2)}) async-start(bf16[8,256,512]{2,1,0:T(8,128)(2,1)} %bitcast.246), calls=%async_computation.1 | async-start | bytes 4194304 | tf_op jit(solution)/shard_map/all_to_all | solution.py:182
  71.5 52.6 %all-to-all-start = ((bf16[8,256,512]{2,1,0:T(8,128)(2,1)}), bf16[8,256,512]{2,1,0:T(8,128)(2,1)S(1)}, u32[]{:S(2)}, u32[]{:S(2)}) async-start(bf16[8,256,512]{2,1,0:T(8,128)(2,1)} %bitcast.245), calls=%async_computation | async-start | bytes 4194304 | tf_op jit(solution)/shard_map/all_to_all | solution.py:181
  124.1 97.6 %all-to-all-start.2 = ((f32[4,512,512]{1,2,0:T(8,128)}), f32[4,512,512]{1,2,0:T(8,128)}, u32[]{:S(2)}, u32[]{:S(2)}) async-start(f32[4,512,512]{1,2,0:T(8,128)} %copy.56), calls=%async_computation.2 | async-start | bytes 8388608 | tf_op jit(solution)/shard_map/all_to_all | solution.py:177
  698.5 53.2 %all-to-all-start.3 = ((bf16[256,8,512]{2,0,1:T(8,128)(2,1)}), bf16[256,8,512]{2,0,1:T(8,128)(2,1)S(1)}, u32[]{:S(2)}, u32[]{:S(2)}) async-start(bf16[256,8,512]{2,0,1:T(8,128)(2,1)} %bitcast.243), calls=%async_computation.3 | async-start | bytes 4194304 | tf_op jit(solution)/shard_map/all_to_all | solution.py:202
  703.4 53.3 %all-gather.2.cloned.1.call-start = ((), (), s32[]{:S(2)}) async-start(), calls=%async_computation.6 | async-start | bytes 6291456 | tf_op jit(solution)/shard_map/all_gather | solution.py:209
  751.7 53.4 %all-to-all-start.4 = ((bf16[256,8,512]{2,0,1:T(8,128)(2,1)}), bf16[256,8,512]{2,0,1:T(8,128)(2,1)}, u32[]{:S(2)}, u32[]{:S(2)}) async-start(bf16[256,8,512]{2,0,1:T(8,128)(2,1)} %bitcast.244), calls=%async_computation.4 | async-start | bytes 4194304 | tf_op jit(solution)/shard_map/all_to_all | solution.py:205
  805.1 131.0 %all-to-all-start.5 = ((f32[512,4,512]{0,2,1:T(8,128)}), f32[512,4,512]{0,2,1:T(8,128)}, u32[]{:S(2)}, u32[]{:S(2)}) async-start(f32[512,4,512]{0,2,1:T(8,128)} %bitcast.235), calls=%async_computation.5 | async-start | bytes 8388608 | tf_op jit(solution)/shard_map/all_to_all | solution.py:210
  920.1 5.6 copy-start.1
  920.1 5.6 copy-start.3
Sparse Core Ops, SparseCore 0:
  706.4 14.8 all-gather.1
where the time goes:
time: 963 us; the launch traced here: 958 us
  matrix products  322 us (33%)
  waiting for transfers between devices  240 us (25%)
  local copies, waits for them, and re-layouts  177 us (18%)
  blocking collectives  97.9 us (10%)
  other arithmetic  70.3 us (7%)
  starting transfers between devices  30.6 us (3%)
  between operations  14.1 us (1%)
    psum x1, blocking collectives, on_device(): grad_skip = lax.psum(gain_term, ('seq', 'dp'))  97.9 us
    all_to_all x1, waiting for transfers between devices, on_device(): lax.all_to_all(long_filter.T, 'seq', split_axis=0, concat_axis=1, tiled=T...  76.2 us
    dynamic_update_slice x96, local copies, waits for them, and re-layouts, run_blocks(): conv_vals, corr_vals, slope = lax.map(one_block, items)  61.4 us
    all_to_all x1, waiting for transfers between devices, on_device(): lax.all_to_all(weighted.T, ('seq', 'dp'), split_axis=0, concat_axis=1, ti...  45.8 us
    all_to_all x1, waiting for transfers between devices, on_device(): lax.all_to_all(to_pieces(corr_vals), ('seq', 'dp'), split_axis=1, concat_...  43 us
    all_to_all x1, waiting for transfers between devices, on_device(): lax.all_to_all(mixed.T, ('seq', 'dp'), split_axis=0, concat_axis=1, tiled...  37.6 us
    all_to_all x1, waiting for transfers between devices, on_device(): lax.all_to_all(to_pieces(conv_vals), ('seq', 'dp'), split_axis=1, concat_...  36.5 us
    while x160, local copies, waits for them, and re-layouts  29.7 us
  transfers between devices with their start and end apart: 7, of which 5 were waited for; matrix products, arithmetic and copies ran while one was open for 8% of the time, Pallas kernels for 0%

commit v1 on v0

--- a/solution.py
+++ b/solution.py
@@ -1,11 +1,422 @@
+import functools
 import math
 
 import jax
 import jax.numpy as jnp
+import ml_dtypes
+import numpy as np
 from jax import lax
+from jax.experimental import pallas as pl
+from jax.experimental.pallas import tpu as pltpu
 from jax.sharding import PartitionSpec as P
 
 full_precision = lax.Precision.HIGHEST
+MESH = pl.DeviceIdType.MESH
+LANES = 128
+INNER = 128
+ROWS = 16
+
+
+def transform_tables(seq_length):
+    full_size = 2 * seq_length
+    outer = full_size // INNER
+    firsts = outer // 2
+    kept = outer // 2 + 1
+    k1 = np.arange(kept)
+    n1 = np.arange(firsts)
+    first = 2.0 * np.pi * (k1[:, None] * n1[None, :] % outer) / outer
+    first_parts = np.stack([np.cos(first), -np.sin(first)], axis=1).reshape(2 * kept, firsts)
+    enter = np.kron(first_parts, np.eye(ROWS))
+    weight = np.where((k1 == 0) | (k1 == outer // 2), 1.0, 2.0) / full_size
+    leave = np.kron((first_parts.reshape(kept, 2, firsts) * weight[:, None, None]).reshape(2 * kept, firsts).T, np.eye(ROWS))
+    n2 = np.arange(INNER)
+    k2 = np.arange(INNER)
+    freq = k1[:, None, None] + outer * k2[None, :, None]
+    angle = 2.0 * np.pi * (freq * n2[None, None, :] % full_size) / full_size
+    cos, sin = np.cos(angle), np.sin(angle)
+    middle = np.concatenate(
+        [np.concatenate([cos, sin], axis=2), np.concatenate([-sin, cos], axis=2)], axis=1
+    )
+    back = np.transpose(middle, (0, 2, 1))
+    return tuple(np.asarray(t).astype(ml_dtypes.bfloat16) for t in (enter, middle, back, leave))
+
+
+def fused_kernel(
+    seq_count, batch_count, factor,
+    q_hbm, k_hbm, v_hbm, ct_hbm, taps_hbm, skip_ref, enter_ref, middle_ref, back_ref, leave_ref,
+    out_hbm, gq_hbm, gk_hbm, gv_hbm, gf_hbm, gs_ref,
+    acts, taps, stage, hstage, xrecv, hrecv, spec, res, sres, rrecv, srecv, gain,
+    in_sem, out_sem, x_send, x_recv, h_send, h_recv, r_send, r_recv, s_send, s_recv, f_send, g_send, g_recv,
+):
+    z = lax.axis_index("seq")
+    b = lax.axis_index("dp")
+    groups = seq_count * batch_count
+    me = z * batch_count + b
+    block_count, rows = acts.shape[1], acts.shape[2]
+    chunks = block_count // groups
+    kept = middle_ref.shape[0]
+    per_row = rows // INNER
+    firsts = seq_count * per_row
+    act_in = (q_hbm, k_hbm, v_hbm, ct_hbm)
+    act_out = (out_hbm, gq_hbm, gk_hbm, gv_hbm)
+
+    def partner(i):
+        pz = lax.rem(z + 1 + i // batch_count, seq_count)
+        pb = lax.rem(b + 1 + lax.rem(i, batch_count), batch_count)
+        return pz, pb, pz * batch_count + pb
+
+    def cols(blk):
+        return pl.ds(pl.multiple_of(blk * LANES, LANES), LANES)
+
+    def start_input(j, carry):
+        c = j // groups
+        _, _, idx = partner(lax.rem(j, groups))
+        blk = c * groups + idx
+        for a in range(4):
+            pltpu.make_async_copy(
+                act_in[a].at[0, :, cols(blk)], acts.at[a, blk], in_sem.at[a, blk]
+            ).start()
+        pltpu.make_async_copy(taps_hbm.at[:, cols(blk)], taps.at[blk], in_sem.at[4, blk]).start()
+        return carry
+
+    lax.fori_loop(0, block_count, start_input, 0)
+
+    barrier = pltpu.get_barrier_semaphore()
+
+    def greet(i, carry):
+        pz, pb, _ = partner(i)
+        pl.semaphore_signal(barrier, inc=1, device_id={"seq": pz, "dp": pb}, device_id_type=MESH)
+        return carry
+
+    lax.fori_loop(0, groups - 1, greet, 0)
+    pl.semaphore_wait(barrier, groups - 1)
+
+    def remote(src, dst, send, recv, pz, pb):
+        return pltpu.make_async_remote_copy(
+            src_ref=src, dst_ref=dst, send_sem=send, recv_sem=recv,
+            device_id={"seq": pz, "dp": pb}, device_id_type=MESH,
+        )
+
+    def send_block(j, carry):
+        c = j // groups
+        pz, pb, idx = partner(lax.rem(j, groups))
+        blk = c * groups + idx
+        for a in range(4):
+            pltpu.make_async_copy(
+                act_in[a].at[0, :, cols(blk)], acts.at[a, blk], in_sem.at[a, blk]
+            ).wait()
+        pltpu.make_async_copy(taps_hbm.at[:, cols(blk)], taps.at[blk], in_sem.at[4, blk]).wait()
+        mixed = (acts[1, blk].astype(jnp.float32) * acts[2, blk].astype(jnp.float32)).astype(jnp.bfloat16)
+        weighted = (acts[3, blk].astype(jnp.float32) * acts[0, blk].astype(jnp.float32)).astype(jnp.bfloat16)
+        stage[blk, 0] = mixed
+        stage[blk, 1] = weighted
+        gain[me, pl.ds(blk, 1), :] = jnp.sum(
+            weighted.astype(jnp.float32) * mixed.astype(jnp.float32), axis=0, keepdims=True
+        )
+
+        @pl.when(idx != me)
+        def _():
+            remote(stage.at[blk], xrecv.at[c, me], x_send.at[blk], x_recv.at[c, me], pz, pb).start()
+
+        @pl.when(idx == me)
+        def _():
+            pltpu.make_async_copy(stage.at[blk], xrecv.at[c, me], x_recv.at[c, me]).start()
+
+        @pl.when(pb == b)
+        def _():
+            hstage[c, pz] = taps[blk].astype(jnp.bfloat16)
+
+            @pl.when(pz != z)
+            def _():
+                remote(hstage.at[c, pz], hrecv.at[c, z], h_send.at[c, pz], h_recv.at[c, z], pz, b).start()
+
+            @pl.when(pz == z)
+            def _():
+                pltpu.make_async_copy(hstage.at[c, pz], hrecv.at[c, z], h_recv.at[c, z]).start()
+
+        return carry
+
+    lax.fori_loop(0, block_count, send_block, 0)
+
+    def send_gain(i, carry):
+        pz, pb, idx = partner(i)
+        remote(gain.at[me], gain.at[me], g_send.at[idx], g_recv.at[me], pz, pb).start()
+        return carry
+
+    lax.fori_loop(0, groups - 1, send_gain, 0)
+
+    def arrived(ref, sem):
+        pltpu.make_async_copy(ref, ref, sem).wait()
+
+    def transform(c, carry):
+        def wait_x(s, inner):
+            arrived(xrecv.at[c, s], x_recv.at[c, s])
+            return inner
+
+        def wait_h(s, inner):
+            arrived(hrecv.at[c, s], h_recv.at[c, s])
+            return inner
+
+        lax.fori_loop(0, groups, wait_x, 0)
+        lax.fori_loop(0, seq_count, wait_h, 0)
+
+        def enter(g, inner):
+            def piece(ref):
+                return jnp.concatenate(
+                    [
+                        ref(n1 // per_row, pl.ds(pl.multiple_of(n1 % per_row * INNER + g * ROWS, ROWS), ROWS))
+                        for n1 in range(firsts)
+                    ],
+                    axis=0,
+                )
+
+            signals = []
+            for a in range(2):
+                for bb in range(batch_count):
+                    signals.append(piece(lambda s, r, a=a, bb=bb: xrecv[c, s * batch_count + bb, a, r, :]))
+            signals.append(piece(lambda s, r: hrecv[c, s, r, :]))
+            stacked = jnp.concatenate(signals, axis=1)
+            grid = jnp.dot(enter_ref[...], stacked, preferred_element_type=jnp.float32).astype(jnp.bfloat16)
+            for k1 in range(kept):
+                for part in range(2):
+                    at = (2 * k1 + part) * ROWS
+                    spec[k1, pl.ds(pl.multiple_of(part * INNER + g * ROWS, ROWS), ROWS), :] = grid[at : at + ROWS]
+            return inner
+
+        lax.fori_loop(0, INNER // ROWS, enter, 0)
+
+        def middle(k1, inner):
+            full = jnp.dot(middle_ref[k1], spec[k1], preferred_element_type=jnp.float32)
+            real, imag = full[:INNER], full[INNER:]
+
+            def take(i):
+                return real[:, i * LANES : (i + 1) * LANES], imag[:, i * LANES : (i + 1) * LANES]
+
+            hr, hi = take(2 * batch_count)
+            out_real, out_imag = [], []
+            for bb in range(batch_count):
+                mr, mi = take(bb)
+                out_real.append(mr * hr - mi * hi)
+                out_imag.append(mr * hi + mi * hr)
+            for bb in range(batch_count):
+                wr, wi = take(batch_count + bb)
+                out_real.append(hr * wr + hi * wi)
+                out_imag.append(hr * wi - hi * wr)
+            slope_real, slope_imag = 0.0, 0.0
+            for bb in range(batch_count):
+                mr, mi = take(bb)
+                wr, wi = take(batch_count + bb)
+                slope_real = slope_real + (mr * wr + mi * wi)
+                slope_imag = slope_imag + (mr * wi - mi * wr)
+            out_real.append(slope_real)
+            out_imag.append(slope_imag)
+            product = jnp.concatenate(
+                [
+                    jnp.concatenate([t.astype(jnp.bfloat16) for t in out_real], axis=1),
+                    jnp.concatenate([t.astype(jnp.bfloat16) for t in out_imag], axis=1),
+                ],
+                axis=0,
+            )
+            spec[k1] = jnp.dot(back_ref[k1], product, preferred_element_type=jnp.float32).astype(jnp.bfloat16)
+            return inner
+
+        lax.fori_loop(0, kept, middle, 0)
+
+        def leave(g, inner):
+            stacked = jnp.concatenate(
+                [
+                    spec[k1, pl.ds(pl.multiple_of(part * INNER + g * ROWS, ROWS), ROWS), :]
+                    for k1 in range(kept)
+                    for part in range(2)
+                ],
+                axis=0,
+            )
+            grid = jnp.dot(leave_ref[...], stacked, preferred_element_type=jnp.float32).astype(jnp.bfloat16)
+            for n1 in range(firsts):
+                s = n1 // per_row
+                r = pl.ds(pl.multiple_of(n1 % per_row * INNER + g * ROWS, ROWS), ROWS)
+                part = grid[n1 * ROWS : (n1 + 1) * ROWS]
+                for bb in range(batch_count):
+                    res[c, s * batch_count + bb, 0, r, :] = part[:, bb * LANES : (bb + 1) * LANES]
+                    at = batch_count + bb
+                    res[c, s * batch_count + bb, 1, r, :] = part[:, at * LANES : (at + 1) * LANES]
+                sres[c, s, r, :] = part[:, 2 * batch_count * LANES :]
+            return inner
+
+        lax.fori_loop(0, INNER // ROWS, leave, 0)
+
+        mine = c * groups + me
+
+        def send_result(i, inner):
+            pz, pb, idx = partner(i)
+
+            @pl.when(jnp.logical_and(pb == b, pz != z))
+            def _():
+                remote(sres.at[c, pz], srecv.at[mine], s_send.at[c, pz], s_recv.at[mine], pz, b).start()
+
+            @pl.when(jnp.logical_and(pb == b, pz == z))
+            def _():
+                pltpu.make_async_copy(sres.at[c, pz], srecv.at[mine], s_recv.at[mine]).start()
+
+            @pl.when(idx != me)
+            def _():
+                remote(res.at[c, idx], rrecv.at[mine], r_send.at[c, idx], r_recv.at[mine], pz, pb).start()
+
+            @pl.when(idx == me)
+            def _():
+                pltpu.make_async_copy(res.at[c, idx], rrecv.at[mine], r_recv.at[mine]).start()
+
+            return inner
+
+        lax.fori_loop(0, groups, send_result, 0)
+        return carry
+
+    lax.fori_loop(0, chunks, transform, 0)
+
+    def finish_chunk(c, carry):
+        def finish_block(i, inner):
+            pz = lax.rem(z + seq_count - i // batch_count, seq_count)
+            pb = lax.rem(b + lax.rem(i, batch_count), batch_count)
+            blk = c * groups + pz * batch_count + pb
+            arrived(rrecv.at[blk], r_recv.at[blk])
+            query = acts[0, blk].astype(jnp.float32)
+            key = acts[1, blk].astype(jnp.float32)
+            value = acts[2, blk].astype(jnp.float32)
+            cot = acts[3, blk].astype(jnp.float32)
+            skip = skip_ref[pl.ds(blk, 1), :]
+            signal = rrecv[blk, 0].astype(jnp.float32) + skip * stage[blk, 0].astype(jnp.float32)
+            back = rrecv[blk, 1].astype(jnp.float32) + skip * stage[blk, 1].astype(jnp.float32)
+            acts[0, blk] = (query * signal).astype(jnp.bfloat16)
+            acts[1, blk] = (cot * signal).astype(jnp.bfloat16)
+            acts[2, blk] = (back * value).astype(jnp.bfloat16)
+            acts[3, blk] = (back * key).astype(jnp.bfloat16)
+            for a in range(4):
+                pltpu.make_async_copy(
+                    acts.at[a, blk], act_out[a].at[0, :, cols(blk)], out_sem.at[a, blk]
+                ).start()
+            arrived(srecv.at[blk], s_recv.at[blk])
+
+            @pl.when(pb == b)
+            def _():
+                remote(srecv.at[blk], srecv.at[blk], f_send.at[c, pz], s_recv.at[blk], z, 1 - b).start()
+
+            taps[blk] = factor * srecv[blk].astype(jnp.float32)
+            pltpu.make_async_copy(taps.at[blk], gf_hbm.at[:, cols(blk)], out_sem.at[4, blk]).start()
+            return inner
+
+        lax.fori_loop(0, groups, finish_block, 0)
+        return carry
+
+    lax.fori_loop(0, chunks, finish_chunk, 0)
+
+    def wait_gain(i, carry):
+        _, _, idx = partner(i)
+        arrived(gain.at[idx], g_recv.at[idx])
+        return carry
+
+    lax.fori_loop(0, groups - 1, wait_gain, 0)
+    total = gain[0]
+    for s in range(1, groups):
+        total = total + gain[s]
+    gs_ref[...] = factor * total
+
+    def drain(j, carry):
+        c = j // groups
+        pz, pb, idx = partner(lax.rem(j, groups))
+        blk = c * groups + idx
+        for a in range(4):
+            pltpu.make_async_copy(
+                acts.at[a, blk], act_out[a].at[0, :, cols(blk)], out_sem.at[a, blk]
+            ).wait()
+        pltpu.make_async_copy(taps.at[blk], gf_hbm.at[:, cols(blk)], out_sem.at[4, blk]).wait()
+
+        @pl.when(idx != me)
+        def _():
+            arrived(stage.at[blk], x_send.at[blk])
+            arrived(res.at[c, idx], r_send.at[c, idx])
+
+        @pl.when(jnp.logical_and(idx != me, c == 0))
+        def _():
+            arrived(gain.at[me], g_send.at[idx])
+
+        @pl.when(pb == b)
+        def _():
+            arrived(srecv.at[blk], f_send.at[c, pz])
+
+            @pl.when(pz != z)
+            def _():
+                arrived(hstage.at[c, pz], h_send.at[c, pz])
+                arrived(sres.at[c, pz], s_send.at[c, pz])
+
+        return carry
+
+    lax.fori_loop(0, block_count, drain, 0)
+
+
+def fused(query_proj, key_proj, value_proj, cotangent, long_filter, skip_gain):
+    rows, width = query_proj.shape[1:]
+    seq_count = lax.axis_size("seq")
+    batch_count = lax.axis_size("dp")
+    groups = seq_count * batch_count
+    seq_length = seq_count * rows
+    block_count = width // LANES
+    chunks = block_count // groups
+    factor = (batch_count * seq_length) ** (-0.5)
+    tables = transform_tables(seq_length)
+    kept = tables[1].shape[0]
+    signals = 2 * batch_count + 1
+    half = jnp.bfloat16
+    dma = pltpu.SemaphoreType.DMA
+    hbm = pl.BlockSpec(memory_space=pl.ANY)
+    vmem = pl.BlockSpec(memory_space=pltpu.VMEM)
+    flops = 2 * chunks * signals * LANES * (2 * tables[0].size * INNER // ROWS + 2 * tables[1].size)
+    results = pl.pallas_call(
+        functools.partial(fused_kernel, seq_count, batch_count, factor),
+        out_shape=[jax.ShapeDtypeStruct((1, rows, width), half)] * 4
+        + [
+            jax.ShapeDtypeStruct((rows, width), jnp.float32),
+            jax.ShapeDtypeStruct((block_count, LANES), jnp.float32),
+        ],
+        in_specs=[hbm] * 5 + [vmem] * 5,
+        out_specs=[hbm] * 5 + [vmem],
+        scratch_shapes=[
+            pltpu.VMEM((4, block_count, rows, LANES), half),
+            pltpu.VMEM((block_count, rows, LANES), jnp.float32),
+            pltpu.VMEM((block_count, 2, rows, LANES), half),
+            pltpu.VMEM((chunks, seq_count, rows, LANES), half),
+            pltpu.VMEM((chunks, groups, 2, rows, LANES), half),
+            pltpu.VMEM((chunks, seq_count, rows, LANES), half),
+            pltpu.VMEM((kept, 2 * INNER, signals * LANES), half),
+            pltpu.VMEM((chunks, groups, 2, rows, LANES), half),
+            pltpu.VMEM((chunks, seq_count, rows, LANES), half),
+            pltpu.VMEM((block_count, 2, rows, LANES), half),
+            pltpu.VMEM((block_count, rows, LANES), half),
+            pltpu.VMEM((groups, block_count, LANES), jnp.float32),
+            dma((5, block_count)),
+            dma((5, block_count)),
+            dma((block_count,)),
+            dma((chunks, groups)),
+            dma((chunks, seq_count)),
+            dma((chunks, seq_count)),
+            dma((chunks, groups)),
+            dma((block_count,)),
+            dma((chunks, seq_count)),
+            dma((block_count,)),
+            dma((chunks, seq_count)),
+            dma((groups,)),
+            dma((groups,)),
+        ],
+        compiler_params=pltpu.CompilerParams(
+            collective_id=0, has_side_effects=True, vmem_limit_bytes=60 * 1024 * 1024
+        ),
+        cost_estimate=pl.CostEstimate(
+            flops=flops, bytes_accessed=24 * rows * width, transcendentals=0
+        ),
+    )(
+        query_proj, key_proj, value_proj, cotangent, long_filter,
+        skip_gain.reshape(block_count, LANES), *(jnp.asarray(t) for t in tables),
+    )
+    return tuple(results[:5]) + (results[5].reshape(width),)
 
 
 def dft_tables(seq_length):
@@ -159,6 +570,13 @@
 
 
 def on_device(query_proj, key_proj, value_proj, cotangent, long_filter, skip_gain):
+    share = query_proj.shape[2] // (lax.axis_size("seq") * lax.axis_size("dp"))
+    if share % LANES == 0 and query_proj.shape[1] % INNER == 0 and lax.axis_size("dp") == 2:
+        return fused(query_proj, key_proj, value_proj, cotangent, long_filter, skip_gain)
+    return spread(query_proj, key_proj, value_proj, cotangent, long_filter, skip_gain)
+
+
+def spread(query_proj, key_proj, value_proj, cotangent, long_filter, skip_gain):
     query_rows = query_proj[0].astype(jnp.float32)
     key_rows = key_proj[0].astype(jnp.float32)
     value_rows = value_proj[0].astype(jnp.float32)

time: 963 us -> 254 us (0.26)
  the two profiles are of different devices: /device:TPU:1 before, /device:TPU:24 now
where the time goes in v1:
time: 254 us
  Pallas kernels  240 us (94%)
  local copies, waits for them, and re-layouts  13.6 us (5%)
    pallas_call x1, Pallas kernels, fused(): pl.pallas_call(functools.partial(fused_kernel, seq_count, batch_count, fa...  240 us
    unnamed x16, local copies, waits for them, and re-layouts  13.6 us

profile of v1, /device:TPU:24, one launch (start us, length us, event | category | flops | bytes accessed | tf_op | source)
XLA Modules:
  0.0 254.0 jit_solution(1651476986711229031)
XLA Ops:
  0.6 239.8 %shard_map.145 = (bf16[1,512,2048]{2,1,0:T(8,128)(2,1)}, bf16[1,512,2048]{2,1,0:T(8,128)(2,1)}, bf16[1,512,2048]{2,1,0:T(8,128)(2,1)}, bf16[1,512,2048]{2,1,0:T(...) custom-call(bf16[1,512,2048]{2,1,0:T(8,128)(2,1)} %q_hbm.1, bf16[1,512,2048]{2,1,0:T(8,128)(2,1)} %k_hbm.1, ...), custom_call_target="tpu_custom_call" | custom-call | flops 11408506880 | bytes 25165824 | tf_op jit(solution)/shard_map/pallas_call | solution.py:373
  240.4 0.0 copy-start.3
  240.4 3.3 %copy.22 = bf16[1,512,2048]{2,1,0:T(8,128)(2,1)} copy(bf16[1,512,2048]{2,1,0:T(8,128)(2,1)} %get-tuple-element.24) | data formatting | bytes 4194304
  243.8 0.0 copy-done.3
  243.8 0.0 copy-start.2
  243.8 1.3 copy.23
  245.1 1.0 copy-done.2
  246.1 0.0 copy-start.1
  246.1 1.3 copy.24
  247.4 1.0 copy-done.1
  248.5 0.0 copy-start
  248.5 1.3 copy.25
  249.8 1.6 copy-done
  251.4 0.0 copy-start.4
  251.4 2.0 copy.26
  253.4 0.0 copy-done.4
  253.4 0.6 copy.27
Async XLA Ops:
  240.4 3.3 %copy-start.3 = (bf16[1,512,2048]{2,1,0:T(8,128)(2,1)S(1)}, bf16[1,512,2048]{2,1,0:T(8,128)(2,1)}, u32[]{:S(2)}) copy-start(bf16[1,512,2048]{2,1,0:T(8,128)(2,1)} %get-tuple-element.25) | copy-start | bytes 6291460
  243.8 2.3 copy-start.2
  246.1 2.3 copy-start.1
  248.5 2.9 %copy-start = (f32[512,2048]{1,0:T(8,128)S(1)}, f32[512,2048]{1,0:T(8,128)}, u32[]{:S(2)}) copy-start(f32[512,2048]{1,0:T(8,128)} %get-tuple-element.28) | copy-start | bytes 12582916
  251.4 2.0 copy-start.4

commit v2 on v1

--- a/solution.py
+++ b/solution.py
@@ -42,21 +42,21 @@
 
 
 def fused_kernel(
-    seq_count, batch_count, factor,
-    q_hbm, k_hbm, v_hbm, ct_hbm, taps_hbm, skip_ref, enter_ref, middle_ref, back_ref, leave_ref,
+    factor,
+    q_hbm, k_hbm, v_hbm, ct_hbm, taps_hbm, skip_ref, enter_ref, middle_ref, back_ref, leave_ref, enter_low_ref, leave_low_ref,
     out_hbm, gq_hbm, gk_hbm, gv_hbm, gf_hbm, gs_ref,
-    acts, taps, stage, hstage, xrecv, hrecv, spec, res, sres, rrecv, srecv, gain,
-    in_sem, out_sem, x_send, x_recv, h_send, h_recv, r_send, r_recv, s_send, s_recv, f_send, g_send, g_recv,
+    acts, taps, stage, hstage, xs, ws, hs, cross, scross, spec, ys, cs, ss, gain,
+    in_sem, out_sem, x_send, x2_send, w_send, h_send, h2_send, f_send, y_send, c_send, s_send, n_send, g_send,
+    x_recv, w_recv, h_recv, cross_recv, scross_recv, y_recv, c_recv, s_recv, g_recv,
 ):
     z = lax.axis_index("seq")
     b = lax.axis_index("dp")
+    seq_count, batch_count = 4, 2
     groups = seq_count * batch_count
     me = z * batch_count + b
     block_count, rows = acts.shape[1], acts.shape[2]
-    chunks = block_count // groups
-    kept = middle_ref.shape[0]
+    steps = block_count // batch_count
     per_row = rows // INNER
-    firsts = seq_count * per_row
     act_in = (q_hbm, k_hbm, v_hbm, ct_hbm)
     act_out = (out_hbm, gq_hbm, gk_hbm, gv_hbm)
 
@@ -68,15 +68,28 @@
     def cols(blk):
         return pl.ds(pl.multiple_of(blk * LANES, LANES), LANES)
 
-    def start_input(j, carry):
-        c = j // groups
-        _, _, idx = partner(lax.rem(j, groups))
-        blk = c * groups + idx
-        for a in range(4):
-            pltpu.make_async_copy(
-                act_in[a].at[0, :, cols(blk)], acts.at[a, blk], in_sem.at[a, blk]
-            ).start()
-        pltpu.make_async_copy(taps_hbm.at[:, cols(blk)], taps.at[blk], in_sem.at[4, blk]).start()
+    def upper_owner(k):
+        return 3 - jnp.minimum(lax.rem(k, 4), 1)
+
+    def input_copies(blk):
+        found = [
+            pltpu.make_async_copy(act_in[a].at[0, :, cols(blk)], acts.at[a, blk], in_sem.at[a, blk])
+            for a in range(4)
+        ]
+        found.append(pltpu.make_async_copy(taps_hbm.at[:, cols(blk)], taps.at[blk], in_sem.at[4, blk]))
+        return found
+
+    def output_copies(blk):
+        found = [
+            pltpu.make_async_copy(acts.at[a, blk], act_out[a].at[0, :, cols(blk)], out_sem.at[a, blk])
+            for a in range(4)
+        ]
+        found.append(pltpu.make_async_copy(taps.at[blk], gf_hbm.at[:, cols(blk)], out_sem.at[4, blk]))
+        return found
+
+    def start_input(blk, carry):
+        for copy in input_copies(blk):
+            copy.start()
         return carry
 
     lax.fori_loop(0, block_count, start_input, 0)
@@ -97,15 +110,86 @@
             device_id={"seq": pz, "dp": pb}, device_id_type=MESH,
         )
 
-    def send_block(j, carry):
-        c = j // groups
-        pz, pb, idx = partner(lax.rem(j, groups))
-        blk = c * groups + idx
-        for a in range(4):
-            pltpu.make_async_copy(
-                act_in[a].at[0, :, cols(blk)], acts.at[a, blk], in_sem.at[a, blk]
-            ).wait()
-        pltpu.make_async_copy(taps_hbm.at[:, cols(blk)], taps.at[blk], in_sem.at[4, blk]).wait()
+    def arrived(ref, sem):
+        pltpu.make_async_copy(ref, ref, sem).wait()
+
+    def move(src, dst, send, recv, pz, pb):
+        here = jnp.logical_and(pz == z, pb == b)
+
+        @pl.when(here)
+        def _():
+            pltpu.make_async_copy(src, dst, recv).start()
+
+        @pl.when(jnp.logical_not(here))
+        def _():
+            remote(src, dst, send, recv, pz, pb).start()
+
+    def settle(src, dst, send, recv, pz, pb):
+        @pl.when(jnp.logical_not(jnp.logical_and(pz == z, pb == b)))
+        def _():
+            arrived(src, send)
+
+    def give_inputs(blk, act):
+        k = blk // batch_count
+        pb = lax.rem(blk, batch_count)
+        owner = upper_owner(k)
+        target = jnp.where(z < 2, 1, owner)
+        slot = lax.rem(z, 2) * batch_count + b
+        act(stage.at[blk, 0], xs.at[k, me], x_send.at[blk], x_recv.at[k, me], target, pb)
+
+        @pl.when(pb == b)
+        def _():
+            act(hstage.at[k], hs.at[k, z], h_send.at[k], h_recv.at[k, z], target, b)
+
+        @pl.when(z == 1)
+        def _():
+            act(stage.at[blk, 0], xs.at[k, me], x2_send.at[blk], x_recv.at[k, me], owner, pb)
+
+            @pl.when(pb == b)
+            def _():
+                act(hstage.at[k], hs.at[k, z], h2_send.at[k], h_recv.at[k, z], owner, b)
+
+        act(stage.at[blk, 1], ws.at[k, slot], w_send.at[blk], w_recv.at[k, slot], target, pb)
+
+    def forward_low(k, act):
+        owner = upper_owner(k)
+        for bb in range(batch_count):
+            act(xs.at[k, bb], xs.at[k, bb], f_send.at[k, bb], x_recv.at[k, bb], owner, b)
+        act(hs.at[k, 0], hs.at[k, 0], f_send.at[k, 2], h_recv.at[k, 0], owner, b)
+
+    def give_upper(k, act):
+        blk = k * batch_count + b
+        for zz in range(2):
+            for bb in range(batch_count):
+                at = zz * batch_count + bb
+                act(xs.at[k, at], cross.at[k, at], c_send.at[k, at], cross_recv.at[k, at], 1, b)
+            act(hs.at[k, zz], scross.at[k, zz], s_send.at[k, zz], scross_recv.at[k, zz], 1, b)
+        for zz in range(2, 4):
+            for bb in range(batch_count):
+                at = zz * batch_count + bb
+                low = at - 2 * batch_count
+                act(ws.at[k, low], ys.at[blk], y_send.at[k, low], y_recv.at[blk], zz, bb)
+                act(xs.at[k, at], cs.at[blk], c_send.at[k, at], c_recv.at[blk], zz, bb)
+            act(hs.at[k, zz], ss.at[blk], s_send.at[k, zz], s_recv.at[blk], zz, b)
+
+    def give_low_conv(k, act):
+        blk = k * batch_count + b
+        for zz in range(2):
+            for bb in range(batch_count):
+                at = zz * batch_count + bb
+                act(ws.at[k, at], ys.at[blk], y_send.at[k, at], y_recv.at[blk], zz, bb)
+
+    def give_low_corr(k, act):
+        blk = k * batch_count + b
+        for zz in range(2):
+            for bb in range(batch_count):
+                at = zz * batch_count + bb
+                act(xs.at[k, 4 + at], cs.at[blk], c_send.at[k, at], c_recv.at[blk], zz, bb)
+            act(hs.at[k, 2 + zz], ss.at[blk], s_send.at[k, zz], s_recv.at[blk], zz, b)
+
+    def send_block(blk, carry):
+        for copy in input_copies(blk):
+            copy.wait()
         mixed = (acts[1, blk].astype(jnp.float32) * acts[2, blk].astype(jnp.float32)).astype(jnp.bfloat16)
         weighted = (acts[3, blk].astype(jnp.float32) * acts[0, blk].astype(jnp.float32)).astype(jnp.bfloat16)
         stage[blk, 0] = mixed
@@ -114,26 +198,11 @@
             weighted.astype(jnp.float32) * mixed.astype(jnp.float32), axis=0, keepdims=True
         )
 
-        @pl.when(idx != me)
+        @pl.when(lax.rem(blk, batch_count) == b)
         def _():
-            remote(stage.at[blk], xrecv.at[c, me], x_send.at[blk], x_recv.at[c, me], pz, pb).start()
-
-        @pl.when(idx == me)
-        def _():
-            pltpu.make_async_copy(stage.at[blk], xrecv.at[c, me], x_recv.at[c, me]).start()
-
-        @pl.when(pb == b)
-        def _():
-            hstage[c, pz] = taps[blk].astype(jnp.bfloat16)
-
-            @pl.when(pz != z)
-            def _():
-                remote(hstage.at[c, pz], hrecv.at[c, z], h_send.at[c, pz], h_recv.at[c, z], pz, b).start()
-
-            @pl.when(pz == z)
-            def _():
-                pltpu.make_async_copy(hstage.at[c, pz], hrecv.at[c, z], h_recv.at[c, z]).start()
-
+            hstage[blk // batch_count] = taps[blk].astype(jnp.bfloat16)
+
+        give_inputs(blk, move)
         return carry
 
     lax.fori_loop(0, block_count, send_block, 0)
@@ -145,20 +214,12 @@
 
     lax.fori_loop(0, groups - 1, send_gain, 0)
 
-    def arrived(ref, sem):
-        pltpu.make_async_copy(ref, ref, sem).wait()
-
-    def transform(c, carry):
-        def wait_x(s, inner):
-            arrived(xrecv.at[c, s], x_recv.at[c, s])
-            return inner
-
-        def wait_h(s, inner):
-            arrived(hrecv.at[c, s], h_recv.at[c, s])
-            return inner
-
-        lax.fori_loop(0, groups, wait_x, 0)
-        lax.fori_loop(0, seq_count, wait_h, 0)
+    def transform(k, low):
+        kept = (middle_ref.shape[0] + 1) // 2 if low else middle_ref.shape[0]
+        firsts = (2 if low else 4) * per_row
+        enter_table = enter_low_ref if low else enter_ref
+        leave_table = leave_low_ref if low else leave_ref
+        scale = 2 if low else 1
 
         def enter(g, inner):
             def piece(ref):
@@ -170,13 +231,20 @@
                     axis=0,
                 )
 
-            signals = []
-            for a in range(2):
-                for bb in range(batch_count):
-                    signals.append(piece(lambda s, r, a=a, bb=bb: xrecv[c, s * batch_count + bb, a, r, :]))
-            signals.append(piece(lambda s, r: hrecv[c, s, r, :]))
+            def weighted_rows(s, r, bb):
+                if low:
+                    return ws[k, s * batch_count + bb, r, :]
+                if s < 2:
+                    return jnp.zeros((ROWS, LANES), jnp.bfloat16)
+                return ws[k, (s - 2) * batch_count + bb, r, :]
+
+            signals = [
+                piece(lambda s, r, bb=bb: xs[k, s * batch_count + bb, r, :]) for bb in range(batch_count)
+            ]
+            signals += [piece(lambda s, r, bb=bb: weighted_rows(s, r, bb)) for bb in range(batch_count)]
+            signals.append(piece(lambda s, r: hs[k, s, r, :]))
             stacked = jnp.concatenate(signals, axis=1)
-            grid = jnp.dot(enter_ref[...], stacked, preferred_element_type=jnp.float32).astype(jnp.bfloat16)
+            grid = jnp.dot(enter_table[...], stacked, preferred_element_type=jnp.float32).astype(jnp.bfloat16)
             for k1 in range(kept):
                 for part in range(2):
                     at = (2 * k1 + part) * ROWS
@@ -186,7 +254,7 @@
         lax.fori_loop(0, INNER // ROWS, enter, 0)
 
         def middle(k1, inner):
-            full = jnp.dot(middle_ref[k1], spec[k1], preferred_element_type=jnp.float32)
+            full = jnp.dot(middle_ref[scale * k1], spec[k1], preferred_element_type=jnp.float32)
             real, imag = full[:INNER], full[INNER:]
 
             def take(i):
@@ -217,7 +285,7 @@
                 ],
                 axis=0,
             )
-            spec[k1] = jnp.dot(back_ref[k1], product, preferred_element_type=jnp.float32).astype(jnp.bfloat16)
+            spec[k1] = jnp.dot(back_ref[scale * k1], product, preferred_element_type=jnp.float32).astype(jnp.bfloat16)
             return inner
 
         lax.fori_loop(0, kept, middle, 0)
@@ -231,87 +299,115 @@
                 ],
                 axis=0,
             )
-            grid = jnp.dot(leave_ref[...], stacked, preferred_element_type=jnp.float32).astype(jnp.bfloat16)
+            grid = jnp.dot(leave_table[...], stacked, preferred_element_type=jnp.float32).astype(jnp.bfloat16)
             for n1 in range(firsts):
                 s = n1 // per_row
                 r = pl.ds(pl.multiple_of(n1 % per_row * INNER + g * ROWS, ROWS), ROWS)
                 part = grid[n1 * ROWS : (n1 + 1) * ROWS]
                 for bb in range(batch_count):
-                    res[c, s * batch_count + bb, 0, r, :] = part[:, bb * LANES : (bb + 1) * LANES]
+                    if low:
+                        ws[k, s * batch_count + bb, r, :] = part[:, bb * LANES : (bb + 1) * LANES]
+                    elif s >= 2:
+                        ws[k, (s - 2) * batch_count + bb, r, :] = part[:, bb * LANES : (bb + 1) * LANES]
                     at = batch_count + bb
-                    res[c, s * batch_count + bb, 1, r, :] = part[:, at * LANES : (at + 1) * LANES]
-                sres[c, s, r, :] = part[:, 2 * batch_count * LANES :]
+                    to = s * batch_count + bb + (4 if low else 0)
+                    xs[k, to, r, :] = part[:, at * LANES : (at + 1) * LANES]
+                hs[k, s + (2 if low else 0), r, :] = part[:, 2 * batch_count * LANES :]
             return inner
 
         lax.fori_loop(0, INNER // ROWS, leave, 0)
 
-        mine = c * groups + me
-
-        def send_result(i, inner):
-            pz, pb, idx = partner(i)
-
-            @pl.when(jnp.logical_and(pb == b, pz != z))
+    def merge_low(k):
+        for zz in range(2):
+            for bb in range(batch_count):
+                at = zz * batch_count + bb
+                arrived(cross.at[k, at], cross_recv.at[k, at])
+                xs[k, 4 + at] = (
+                    xs[k, 4 + at].astype(jnp.float32) + cross[k, at].astype(jnp.float32)
+                ).astype(jnp.bfloat16)
+            arrived(scross.at[k, zz], scross_recv.at[k, zz])
+            hs[k, 2 + zz] = (
+                hs[k, 2 + zz].astype(jnp.float32) + scross[k, zz].astype(jnp.float32)
+            ).astype(jnp.bfloat16)
+        give_low_corr(k, move)
+
+    lag = 4
+
+    @pl.when(z == 1)
+    def _():
+        def step(k, carry):
+            @pl.when(k < steps)
             def _():
-                remote(sres.at[c, pz], srecv.at[mine], s_send.at[c, pz], s_recv.at[mine], pz, b).start()
-
-            @pl.when(jnp.logical_and(pb == b, pz == z))
+                for s in range(4):
+                    arrived(xs.at[k, s], x_recv.at[k, s])
+                for s in range(2):
+                    arrived(hs.at[k, s], h_recv.at[k, s])
+                forward_low(k, move)
+                for s in range(4):
+                    arrived(ws.at[k, s], w_recv.at[k, s])
+                transform(k, True)
+                give_low_conv(k, move)
+
+            @pl.when(k >= lag)
             def _():
-                pltpu.make_async_copy(sres.at[c, pz], srecv.at[mine], s_recv.at[mine]).start()
-
-            @pl.when(idx != me)
+                merge_low(k - lag)
+
+            return carry
+
+        lax.fori_loop(0, steps + lag, step, 0)
+
+    @pl.when(z >= 2)
+    def _():
+        def step(k, carry):
+            @pl.when(upper_owner(k) == z)
             def _():
-                remote(res.at[c, idx], rrecv.at[mine], r_send.at[c, idx], r_recv.at[mine], pz, pb).start()
-
-            @pl.when(idx == me)
-            def _():
-                pltpu.make_async_copy(res.at[c, idx], rrecv.at[mine], r_recv.at[mine]).start()
-
-            return inner
-
-        lax.fori_loop(0, groups, send_result, 0)
+                for s in range(8):
+                    arrived(xs.at[k, s], x_recv.at[k, s])
+                for s in range(4):
+                    arrived(hs.at[k, s], h_recv.at[k, s])
+                    arrived(ws.at[k, s], w_recv.at[k, s])
+                transform(k, False)
+                give_upper(k, move)
+
+            return carry
+
+        lax.fori_loop(0, steps, step, 0)
+
+    def finish_block(blk, carry):
+        k = blk // batch_count
+        pb = lax.rem(blk, batch_count)
+        arrived(ys.at[blk], y_recv.at[blk])
+        arrived(cs.at[blk], c_recv.at[blk])
+        query = acts[0, blk].astype(jnp.float32)
+        key = acts[1, blk].astype(jnp.float32)
+        value = acts[2, blk].astype(jnp.float32)
+        cot = acts[3, blk].astype(jnp.float32)
+        skip = skip_ref[pl.ds(blk, 1), :]
+        signal = ys[blk].astype(jnp.float32) + skip * stage[blk, 0].astype(jnp.float32)
+        back = cs[blk].astype(jnp.float32) + skip * stage[blk, 1].astype(jnp.float32)
+        acts[0, blk] = (query * signal).astype(jnp.bfloat16)
+        acts[1, blk] = (cot * signal).astype(jnp.bfloat16)
+        acts[2, blk] = (back * value).astype(jnp.bfloat16)
+        acts[3, blk] = (back * key).astype(jnp.bfloat16)
+        copies = output_copies(blk)
+        for copy in copies[:4]:
+            copy.start()
+        arrived(ss.at[blk], s_recv.at[blk])
+
+        @pl.when(pb == b)
+        def _():
+            remote(ss.at[blk], ss.at[blk], n_send.at[k], s_recv.at[blk], z, 1 - b).start()
+
+        taps[blk] = factor * ss[blk].astype(jnp.float32)
+        copies[4].start()
         return carry
 
-    lax.fori_loop(0, chunks, transform, 0)
-
-    def finish_chunk(c, carry):
-        def finish_block(i, inner):
-            pz = lax.rem(z + seq_count - i // batch_count, seq_count)
-            pb = lax.rem(b + lax.rem(i, batch_count), batch_count)
-            blk = c * groups + pz * batch_count + pb
-            arrived(rrecv.at[blk], r_recv.at[blk])
-            query = acts[0, blk].astype(jnp.float32)
-            key = acts[1, blk].astype(jnp.float32)
-            value = acts[2, blk].astype(jnp.float32)
-            cot = acts[3, blk].astype(jnp.float32)
-            skip = skip_ref[pl.ds(blk, 1), :]
-            signal = rrecv[blk, 0].astype(jnp.float32) + skip * stage[blk, 0].astype(jnp.float32)
-            back = rrecv[blk, 1].astype(jnp.float32) + skip * stage[blk, 1].astype(jnp.float32)
-            acts[0, blk] = (query * signal).astype(jnp.bfloat16)
-            acts[1, blk] = (cot * signal).astype(jnp.bfloat16)
-            acts[2, blk] = (back * value).astype(jnp.bfloat16)
-            acts[3, blk] = (back * key).astype(jnp.bfloat16)
-            for a in range(4):
-                pltpu.make_async_copy(
-                    acts.at[a, blk], act_out[a].at[0, :, cols(blk)], out_sem.at[a, blk]
-                ).start()
-            arrived(srecv.at[blk], s_recv.at[blk])
-
-            @pl.when(pb == b)
-            def _():
-                remote(srecv.at[blk], srecv.at[blk], f_send.at[c, pz], s_recv.at[blk], z, 1 - b).start()
-
-            taps[blk] = factor * srecv[blk].astype(jnp.float32)
-            pltpu.make_async_copy(taps.at[blk], gf_hbm.at[:, cols(blk)], out_sem.at[4, blk]).start()
-            return inner
-
-        lax.fori_loop(0, groups, finish_block, 0)
-        return carry
-
-    lax.fori_loop(0, chunks, finish_chunk, 0)
+    lax.fori_loop(0, block_count, finish_block, 0)
 
     def wait_gain(i, carry):
         _, _, idx = partner(i)
         arrived(gain.at[idx], g_recv.at[idx])
+        arrived(gain.at[me], g_send.at[idx])
         return carry
 
     lax.fori_loop(0, groups - 1, wait_gain, 0)
@@ -320,33 +416,25 @@
         total = total + gain[s]
     gs_ref[...] = factor * total
 
-    def drain(j, carry):
-        c = j // groups
-        pz, pb, idx = partner(lax.rem(j, groups))
-        blk = c * groups + idx
-        for a in range(4):
-            pltpu.make_async_copy(
-                acts.at[a, blk], act_out[a].at[0, :, cols(blk)], out_sem.at[a, blk]
-            ).wait()
-        pltpu.make_async_copy(taps.at[blk], gf_hbm.at[:, cols(blk)], out_sem.at[4, blk]).wait()
-
-        @pl.when(idx != me)
+    def drain(blk, carry):
+        for copy in output_copies(blk):
+            copy.wait()
+        give_inputs(blk, settle)
+        k = blk // batch_count
+
+        @pl.when(lax.rem(blk, batch_count) == b)
         def _():
-            arrived(stage.at[blk], x_send.at[blk])
-            arrived(res.at[c, idx], r_send.at[c, idx])
-
-        @pl.when(jnp.logical_and(idx != me, c == 0))
-        def _():
-            arrived(gain.at[me], g_send.at[idx])
-
-        @pl.when(pb == b)
-        def _():
-            arrived(srecv.at[blk], f_send.at[c, pz])
-
-            @pl.when(pz != z)
+            arrived(ss.at[blk], n_send.at[k])
+
+            @pl.when(z == 1)
             def _():
-                arrived(hstage.at[c, pz], h_send.at[c, pz])
-                arrived(sres.at[c, pz], s_send.at[c, pz])
+                forward_low(k, settle)
+                give_low_conv(k, settle)
+                give_low_corr(k, settle)
+
+            @pl.when(upper_owner(k) == z)
+            def _():
+                give_upper(k, settle)
 
         return carry
 
@@ -360,54 +448,67 @@
     groups = seq_count * batch_count
     seq_length = seq_count * rows
     block_count = width // LANES
-    chunks = block_count // groups
+    steps = block_count // batch_count
     factor = (batch_count * seq_length) ** (-0.5)
     tables = transform_tables(seq_length)
+    low_tables = transform_tables(seq_length // 2)
+    tables = tables + (low_tables[0], low_tables[3])
     kept = tables[1].shape[0]
     signals = 2 * batch_count + 1
     half = jnp.bfloat16
     dma = pltpu.SemaphoreType.DMA
     hbm = pl.BlockSpec(memory_space=pl.ANY)
     vmem = pl.BlockSpec(memory_space=pltpu.VMEM)
-    flops = 2 * chunks * signals * LANES * (2 * tables[0].size * INNER // ROWS + 2 * tables[1].size)
+    flops = 2 * steps * signals * LANES * (2 * tables[0].size * INNER // ROWS + 2 * tables[1].size)
     results = pl.pallas_call(
-        functools.partial(fused_kernel, seq_count, batch_count, factor),
+        functools.partial(fused_kernel, factor),
         out_shape=[jax.ShapeDtypeStruct((1, rows, width), half)] * 4
         + [
             jax.ShapeDtypeStruct((rows, width), jnp.float32),
             jax.ShapeDtypeStruct((block_count, LANES), jnp.float32),
         ],
-        in_specs=[hbm] * 5 + [vmem] * 5,
+        in_specs=[hbm] * 5 + [vmem] * 7,
         out_specs=[hbm] * 5 + [vmem],
         scratch_shapes=[
             pltpu.VMEM((4, block_count, rows, LANES), half),
             pltpu.VMEM((block_count, rows, LANES), jnp.float32),
             pltpu.VMEM((block_count, 2, rows, LANES), half),
-            pltpu.VMEM((chunks, seq_count, rows, LANES), half),
-            pltpu.VMEM((chunks, groups, 2, rows, LANES), half),
-            pltpu.VMEM((chunks, seq_count, rows, LANES), half),
+            pltpu.VMEM((steps, rows, LANES), half),
+            pltpu.VMEM((steps, groups, rows, LANES), half),
+            pltpu.VMEM((steps, groups // 2, rows, LANES), half),
+            pltpu.VMEM((steps, seq_count, rows, LANES), half),
+            pltpu.VMEM((steps, groups // 2, rows, LANES), half),
+            pltpu.VMEM((steps, seq_count // 2, rows, LANES), half),
             pltpu.VMEM((kept, 2 * INNER, signals * LANES), half),
-            pltpu.VMEM((chunks, groups, 2, rows, LANES), half),
-            pltpu.VMEM((chunks, seq_count, rows, LANES), half),
-            pltpu.VMEM((block_count, 2, rows, LANES), half),
+            pltpu.VMEM((block_count, rows, LANES), half),
+            pltpu.VMEM((block_count, rows, LANES), half),
             pltpu.VMEM((block_count, rows, LANES), half),
             pltpu.VMEM((groups, block_count, LANES), jnp.float32),
             dma((5, block_count)),
             dma((5, block_count)),
             dma((block_count,)),
-            dma((chunks, groups)),
-            dma((chunks, seq_count)),
-            dma((chunks, seq_count)),
-            dma((chunks, groups)),
             dma((block_count,)),
-            dma((chunks, seq_count)),
             dma((block_count,)),
-            dma((chunks, seq_count)),
+            dma((steps,)),
+            dma((steps,)),
+            dma((steps, 3)),
+            dma((steps, groups // 2)),
+            dma((steps, groups)),
+            dma((steps, seq_count)),
+            dma((steps,)),
             dma((groups,)),
+            dma((steps, groups)),
+            dma((steps, groups // 2)),
+            dma((steps, seq_count)),
+            dma((steps, groups // 2)),
+            dma((steps, seq_count // 2)),
+            dma((block_count,)),
+            dma((block_count,)),
+            dma((block_count,)),
             dma((groups,)),
         ],
         compiler_params=pltpu.CompilerParams(
-            collective_id=0, has_side_effects=True, vmem_limit_bytes=60 * 1024 * 1024
+            collective_id=0, has_side_effects=True, vmem_limit_bytes=62 * 1024 * 1024
         ),
         cost_estimate=pl.CostEstimate(
             flops=flops, bytes_accessed=24 * rows * width, transcendentals=0
@@ -570,8 +671,9 @@
 
 
 def on_device(query_proj, key_proj, value_proj, cotangent, long_filter, skip_gain):
-    share = query_proj.shape[2] // (lax.axis_size("seq") * lax.axis_size("dp"))
-    if share % LANES == 0 and query_proj.shape[1] % INNER == 0 and lax.axis_size("dp") == 2:
+    rows, width = query_proj.shape[1:]
+    grouped = lax.axis_size("seq") == 4 and lax.axis_size("dp") == 2
+    if grouped and rows % INNER == 0 and width % (2 * LANES) == 0 and rows * width <= 2**20:
         return fused(query_proj, key_proj, value_proj, cotangent, long_filter, skip_gain)
     return spread(query_proj, key_proj, value_proj, cotangent, long_filter, skip_gain)
 

time: 254 us -> 280 us (1.10)
  the two profiles are of different devices: /device:TPU:24 before, /device:TPU:12 now
where the time goes in v2:
time: 280 us
  Pallas kernels  266 us (95%)
  local copies, waits for them, and re-layouts  13.6 us (5%)
    pallas_call x1, Pallas kernels, fused(): pl.pallas_call(functools.partial(fused_kernel, factor), out_shape=[jax.Sh...  266 us
    unnamed x16, local copies, waits for them, and re-layouts  13.6 us

profile of v2, /device:TPU:12, one launch (start us, length us, event | category | flops | bytes accessed | tf_op | source)
XLA Modules:
  0.0 280.1 jit_solution(10075389077631510560)
XLA Ops:
  0.6 265.9 %shard_map.163 = (bf16[1,512,2048]{2,1,0:T(8,128)(2,1)}, bf16[1,512,2048]{2,1,0:T(8,128)(2,1)}, bf16[1,512,2048]{2,1,0:T(8,128)(2,1)}, bf16[1,512,2048]{2,1,0:T(...) custom-call(bf16[1,512,2048]{2,1,0:T(8,128)(2,1)} %q_hbm.1, bf16[1,512,2048]{2,1,0:T(8,128)(2,1)} %k_hbm.1, ...), custom_call_target="tpu_custom_call" | custom-call | flops 45634027520 | bytes 25165824 | tf_op jit(solution)/shard_map/pallas_call | solution.py:463
  266.5 0.0 copy-start.3
  266.5 3.3 %copy.24 = bf16[1,512,2048]{2,1,0:T(8,128)(2,1)} copy(bf16[1,512,2048]{2,1,0:T(8,128)(2,1)} %get-tuple-element.24) | data formatting | bytes 4194304
  269.8 0.0 copy-done.3
  269.8 0.0 copy-start.2
  269.8 1.3 copy.25
  271.1 1.0 copy-done.2
  272.2 0.0 copy-start.1
  272.2 1.3 copy.26
  273.5 1.0 copy-done.1
  274.5 0.0 copy-start
  274.5 1.3 copy.27
  275.8 1.6 copy-done
  277.5 0.0 copy-start.4
  277.5 2.0 copy.28
  279.5 0.0 copy-done.4
  279.5 0.6 copy.29
Async XLA Ops:
  266.5 3.3 %copy-start.3 = (bf16[1,512,2048]{2,1,0:T(8,128)(2,1)S(1)}, bf16[1,512,2048]{2,1,0:T(8,128)(2,1)}, u32[]{:S(2)}) copy-start(bf16[1,512,2048]{2,1,0:T(8,128)(2,1)} %get-tuple-element.25) | copy-start | bytes 6291460
  269.8 2.3 copy-start.2
  272.2 2.3 copy-start.1
  274.5 2.9 %copy-start = (f32[512,2048]{1,0:T(8,128)S(1)}, f32[512,2048]{1,0:T(8,128)}, u32[]{:S(2)}) copy-start(f32[512,2048]{1,0:T(8,128)} %get-tuple-element.28) | copy-start | bytes 12582916
  277.5 2.0 copy-start.4

commit v3 on v2

--- a/solution.py
+++ b/solution.py
@@ -26,9 +26,11 @@
     n1 = np.arange(firsts)
     first = 2.0 * np.pi * (k1[:, None] * n1[None, :] % outer) / outer
     first_parts = np.stack([np.cos(first), -np.sin(first)], axis=1).reshape(2 * kept, firsts)
-    enter = np.kron(first_parts, np.eye(ROWS))
+    live = np.ones(2 * kept, bool)
+    live[[1, 2 * kept - 1]] = False
+    enter = np.kron(first_parts[live], np.eye(ROWS))
     weight = np.where((k1 == 0) | (k1 == outer // 2), 1.0, 2.0) / full_size
-    leave = np.kron((first_parts.reshape(kept, 2, firsts) * weight[:, None, None]).reshape(2 * kept, firsts).T, np.eye(ROWS))
+    leave = np.kron((first_parts.reshape(kept, 2, firsts) * weight[:, None, None]).reshape(2 * kept, firsts)[live].T, np.eye(ROWS))
     n2 = np.arange(INNER)
     k2 = np.arange(INNER)
     freq = k1[:, None, None] + outer * k2[None, :, None]
@@ -69,7 +71,14 @@
         return pl.ds(pl.multiple_of(blk * LANES, LANES), LANES)
 
     def upper_owner(k):
-        return 3 - jnp.minimum(lax.rem(k, 4), 1)
+        return jnp.where(jnp.logical_or(k == 1, k == 3), 3, 2)
+
+    def merge_order(m):
+        order = [0, 2, 4, 5, 1, 3] + list(range(6, steps))
+        k = 0
+        for i, step in enumerate(order):
+            k = k + jnp.where(m == i, step, 0)
+        return k
 
     def input_copies(blk):
         found = [
@@ -141,15 +150,14 @@
         def _():
             act(hstage.at[k], hs.at[k, z], h_send.at[k], h_recv.at[k, z], target, b)
 
-        @pl.when(z == 1)
-        def _():
+        act(stage.at[blk, 1], ws.at[k, slot], w_send.at[blk], w_recv.at[k, slot], target, pb)
+
+    def give_across(k, act):
+        owner = upper_owner(k)
+        for pb in range(batch_count):
+            blk = k * batch_count + pb
             act(stage.at[blk, 0], xs.at[k, me], x2_send.at[blk], x_recv.at[k, me], owner, pb)
-
-            @pl.when(pb == b)
-            def _():
-                act(hstage.at[k], hs.at[k, z], h2_send.at[k], h_recv.at[k, z], owner, b)
-
-        act(stage.at[blk, 1], ws.at[k, slot], w_send.at[blk], w_recv.at[k, slot], target, pb)
+        act(hstage.at[k], hs.at[k, z], h2_send.at[k], h_recv.at[k, z], owner, b)
 
     def forward_low(k, act):
         owner = upper_owner(k)
@@ -187,6 +195,8 @@
                 act(xs.at[k, 4 + at], cs.at[blk], c_send.at[k, at], c_recv.at[blk], zz, bb)
             act(hs.at[k, 2 + zz], ss.at[blk], s_send.at[k, zz], s_recv.at[blk], zz, b)
 
+    ahead = 2
+
     def send_block(blk, carry):
         for copy in input_copies(blk):
             copy.wait()
@@ -203,6 +213,11 @@
             hstage[blk // batch_count] = taps[blk].astype(jnp.bfloat16)
 
         give_inputs(blk, move)
+
+        @pl.when(jnp.logical_and(z == 1, jnp.logical_and(lax.rem(blk, 2) == 1, blk < 2 * ahead)))
+        def _():
+            give_across(blk // batch_count, move)
+
         return carry
 
     lax.fori_loop(0, block_count, send_block, 0)
@@ -220,6 +235,9 @@
         enter_table = enter_low_ref if low else enter_ref
         leave_table = leave_low_ref if low else leave_ref
         scale = 2 if low else 1
+        live = [(k1, part) for k1 in range(kept) for part in range(2) if part == 0 or 0 < k1 < kept - 1]
+        for k1 in (0, kept - 1):
+            spec[k1, INNER:, :] = jnp.zeros((INNER, spec.shape[2]), jnp.bfloat16)
 
         def enter(g, inner):
             def piece(ref):
@@ -245,16 +263,14 @@
             signals.append(piece(lambda s, r: hs[k, s, r, :]))
             stacked = jnp.concatenate(signals, axis=1)
             grid = jnp.dot(enter_table[...], stacked, preferred_element_type=jnp.float32).astype(jnp.bfloat16)
-            for k1 in range(kept):
-                for part in range(2):
-                    at = (2 * k1 + part) * ROWS
-                    spec[k1, pl.ds(pl.multiple_of(part * INNER + g * ROWS, ROWS), ROWS), :] = grid[at : at + ROWS]
+            for i, (k1, part) in enumerate(live):
+                at = i * ROWS
+                spec[k1, pl.ds(pl.multiple_of(part * INNER + g * ROWS, ROWS), ROWS), :] = grid[at : at + ROWS]
             return inner
 
         lax.fori_loop(0, INNER // ROWS, enter, 0)
 
-        def middle(k1, inner):
-            full = jnp.dot(middle_ref[scale * k1], spec[k1], preferred_element_type=jnp.float32)
+        def products(full):
             real, imag = full[:INNER], full[INNER:]
 
             def take(i):
@@ -278,24 +294,38 @@
                 slope_imag = slope_imag + (mr * wi - mi * wr)
             out_real.append(slope_real)
             out_imag.append(slope_imag)
-            product = jnp.concatenate(
+            return jnp.concatenate(
                 [
                     jnp.concatenate([t.astype(jnp.bfloat16) for t in out_real], axis=1),
                     jnp.concatenate([t.astype(jnp.bfloat16) for t in out_imag], axis=1),
                 ],
                 axis=0,
             )
-            spec[k1] = jnp.dot(back_ref[scale * k1], product, preferred_element_type=jnp.float32).astype(jnp.bfloat16)
+
+        def middle(firsts_now):
+            fulls = [
+                jnp.dot(middle_ref[scale * k1], spec[k1], preferred_element_type=jnp.float32) for k1 in firsts_now
+            ]
+            turned = [products(full) for full in fulls]
+            backs = [
+                jnp.dot(back_ref[scale * k1], turn, preferred_element_type=jnp.float32).astype(jnp.bfloat16)
+                for k1, turn in zip(firsts_now, turned)
+            ]
+            for k1, back in zip(firsts_now, backs):
+                spec[k1] = back
+
+        def middle_pair(p, inner):
+            middle([2 * p, 2 * p + 1])
             return inner
 
-        lax.fori_loop(0, kept, middle, 0)
+        lax.fori_loop(0, kept // 2, middle_pair, 0)
+        middle([kept - 1])
 
         def leave(g, inner):
             stacked = jnp.concatenate(
                 [
                     spec[k1, pl.ds(pl.multiple_of(part * INNER + g * ROWS, ROWS), ROWS), :]
-                    for k1 in range(kept)
-                    for part in range(2)
+                    for k1, part in live
                 ],
                 axis=0,
             )
@@ -330,48 +360,6 @@
                 hs[k, 2 + zz].astype(jnp.float32) + scross[k, zz].astype(jnp.float32)
             ).astype(jnp.bfloat16)
         give_low_corr(k, move)
-
-    lag = 4
-
-    @pl.when(z == 1)
-    def _():
-        def step(k, carry):
-            @pl.when(k < steps)
-            def _():
-                for s in range(4):
-                    arrived(xs.at[k, s], x_recv.at[k, s])
-                for s in range(2):
-                    arrived(hs.at[k, s], h_recv.at[k, s])
-                forward_low(k, move)
-                for s in range(4):
-                    arrived(ws.at[k, s], w_recv.at[k, s])
-                transform(k, True)
-                give_low_conv(k, move)
-
-            @pl.when(k >= lag)
-            def _():
-                merge_low(k - lag)
-
-            return carry
-
-        lax.fori_loop(0, steps + lag, step, 0)
-
-    @pl.when(z >= 2)
-    def _():
-        def step(k, carry):
-            @pl.when(upper_owner(k) == z)
-            def _():
-                for s in range(8):
-                    arrived(xs.at[k, s], x_recv.at[k, s])
-                for s in range(4):
-                    arrived(hs.at[k, s], h_recv.at[k, s])
-                    arrived(ws.at[k, s], w_recv.at[k, s])
-                transform(k, False)
-                give_upper(k, move)
-
-            return carry
-
-        lax.fori_loop(0, steps, step, 0)
 
     def finish_block(blk, carry):
         k = blk // batch_count
@@ -402,7 +390,80 @@
         copies[4].start()
         return carry
 
-    lax.fori_loop(0, block_count, finish_block, 0)
+    def finish_step(k):
+        for bb in range(batch_count):
+            finish_block(k * batch_count + lax.rem(b + bb, batch_count), 0)
+
+    def finish_rest(m, carry):
+        finish_step(merge_order(m))
+        return carry
+
+    lag = 5
+    wait_upper = 4
+
+    @pl.when(z == 0)
+    def _():
+        lax.fori_loop(0, steps, finish_rest, 0)
+
+    @pl.when(z == 1)
+    def _():
+        def step(k, carry):
+            @pl.when(k < steps)
+            def _():
+                for s in range(4):
+                    arrived(xs.at[k, s], x_recv.at[k, s])
+                for s in range(2):
+                    arrived(hs.at[k, s], h_recv.at[k, s])
+                forward_low(k, move)
+
+                @pl.when(k < steps - ahead)
+                def _():
+                    give_across(k + ahead, move)
+
+                for s in range(4):
+                    arrived(ws.at[k, s], w_recv.at[k, s])
+                transform(k, True)
+                give_low_conv(k, move)
+
+            @pl.when(k >= lag)
+            def _():
+                merge_low(merge_order(k - lag))
+
+            @pl.when(k >= lag + 1)
+            def _():
+                finish_step(merge_order(k - lag - 1))
+
+            return carry
+
+        lax.fori_loop(0, steps + lag, step, 0)
+        finish_step(merge_order(steps - 1))
+
+    @pl.when(z >= 2)
+    def _():
+        def step(k, carry):
+            @pl.when(upper_owner(k) == z)
+            def _():
+                for s in range(8):
+                    arrived(xs.at[k, s], x_recv.at[k, s])
+                for s in range(4):
+                    arrived(hs.at[k, s], h_recv.at[k, s])
+                    arrived(ws.at[k, s], w_recv.at[k, s])
+                transform(k, False)
+                give_upper(k, move)
+
+            @pl.when(k >= wait_upper)
+            def _():
+                finish_step(merge_order(k - wait_upper))
+
+            return carry
+
+        lax.fori_loop(0, steps, step, 0)
+
+        def rest(m, carry):
+            finish_step(merge_order(m))
+            return carry
+
+        lax.fori_loop(steps - wait_upper, steps, rest, 0)
 
     def wait_gain(i, carry):
         _, _, idx = partner(i)
@@ -428,6 +489,7 @@
 
             @pl.when(z == 1)
             def _():
+                give_across(k, settle)
                 forward_low(k, settle)
                 give_low_conv(k, settle)
                 give_low_corr(k, settle)
@@ -673,7 +735,7 @@
 def on_device(query_proj, key_proj, value_proj, cotangent, long_filter, skip_gain):
     rows, width = query_proj.shape[1:]
     grouped = lax.axis_size("seq") == 4 and lax.axis_size("dp") == 2
-    if grouped and rows % INNER == 0 and width % (2 * LANES) == 0 and rows * width <= 2**20:
+    if grouped and rows % INNER == 0 and width >= 16 * LANES and width % (2 * LANES) == 0 and rows * width <= 2**20:
         return fused(query_proj, key_proj, value_proj, cotangent, long_filter, skip_gain)
     return spread(query_proj, key_proj, value_proj, cotangent, long_filter, skip_gain)
 

time: 280 us -> 234 us (0.84)
  the two profiles are of different devices: /device:TPU:12 before, /device:TPU:1 now
where the time goes in v3:
time: 234 us
  Pallas kernels  220 us (94%)
  local copies, waits for them, and re-layouts  13.6 us (6%)
    pallas_call x1, Pallas kernels, fused(): pl.pallas_call(functools.partial(fused_kernel, factor), out_shape=[jax.Sh...  220 us
    unnamed x16, local copies, waits for them, and re-layouts  13.6 us

profile of v3, /device:TPU:1, one launch (start us, length us, event | category | flops | bytes accessed | tf_op | source)
XLA Modules:
  0.0 234.2 jit_solution(16562552660794736412)
XLA Ops:
  0.6 220.0 %shard_map.163 = (bf16[1,512,2048]{2,1,0:T(8,128)(2,1)}, bf16[1,512,2048]{2,1,0:T(8,128)(2,1)}, bf16[1,512,2048]{2,1,0:T(8,128)(2,1)}, bf16[1,512,2048]{2,1,0:T(...) custom-call(bf16[1,512,2048]{2,1,0:T(8,128)(2,1)} %q_hbm.1, bf16[1,512,2048]{2,1,0:T(8,128)(2,1)} %k_hbm.1, ...), custom_call_target="tpu_custom_call" | custom-call | flops 44291850240 | bytes 25165824 | tf_op jit(solution)/shard_map/pallas_call | solution.py:525
  220.7 0.0 copy-start.3
  220.7 3.3 %copy.24 = bf16[1,512,2048]{2,1,0:T(8,128)(2,1)} copy(bf16[1,512,2048]{2,1,0:T(8,128)(2,1)} %get-tuple-element.24) | data formatting | bytes 4194304
  224.0 0.0 copy-done.3
  224.0 0.0 copy-start.2
  224.0 1.3 copy.25
  225.3 1.0 copy-done.2
  226.3 0.0 copy-start.1
  226.3 1.3 copy.26
  227.7 1.0 copy-done.1
  228.7 0.0 copy-start
  228.7 1.3 copy.27
  230.0 1.6 copy-done
  231.6 0.0 copy-start.4
  231.6 2.0 copy.28
  233.6 0.0 copy-done.4
  233.6 0.6 copy.29
Async XLA Ops:
  220.7 3.3 %copy-start.3 = (bf16[1,512,2048]{2,1,0:T(8,128)(2,1)S(1)}, bf16[1,512,2048]{2,1,0:T(8,128)(2,1)}, u32[]{:S(2)}) copy-start(bf16[1,512,2048]{2,1,0:T(8,128)(2,1)} %get-tuple-element.25) | copy-start | bytes 6291460
  224.0 2.3 %copy-start.2 = (bf16[1,512,2048]{2,1,0:T(8,128)(2,1)S(1)}, bf16[1,512,2048]{2,1,0:T(8,128)(2,1)}, u32[]{:S(2)}) copy-start(bf16[1,512,2048]{2,1,0:T(8,128)(2,1)} %get-tuple-element.26) | copy-start | bytes 6291460
  226.3 2.3 %copy-start.1 = (bf16[1,512,2048]{2,1,0:T(8,128)(2,1)S(1)}, bf16[1,512,2048]{2,1,0:T(8,128)(2,1)}, u32[]{:S(2)}) copy-start(bf16[1,512,2048]{2,1,0:T(8,128)(2,1)} %get-tuple-element.27) | copy-start | bytes 6291460
  228.7 2.9 %copy-start = (f32[512,2048]{1,0:T(8,128)S(1)}, f32[512,2048]{1,0:T(8,128)}, u32[]{:S(2)}) copy-start(f32[512,2048]{1,0:T(8,128)} %get-tuple-element.28) | copy-start | bytes 12582916
  231.6 2.0 copy-start.4

commit v4 on v3

--- a/solution.py
+++ b/solution.py
@@ -71,10 +71,10 @@
         return pl.ds(pl.multiple_of(blk * LANES, LANES), LANES)
 
     def upper_owner(k):
-        return jnp.where(jnp.logical_or(k == 1, k == 3), 3, 2)
+        return jnp.where(jnp.logical_and(lax.rem(k, 2) == 1, k < 6), 3, 2)
 
     def merge_order(m):
-        order = [0, 2, 4, 5, 1, 3] + list(range(6, steps))
+        order = [0, 2, 4, 6, 1, 3, 5, 7] + list(range(8, steps))
         k = 0
         for i, step in enumerate(order):
             k = k + jnp.where(m == i, step, 0)

time: 234 us -> 248 us (1.060)
  Pallas kernels: 220 us -> 234 us
    pallas_call x1, Pallas kernels: 220 us -> 234 us  [fused(): pl.pallas_call(functools.partial(fused_kernel, factor), out_shape=[jax.Sh...]
where the time goes in v4:
time: 248 us
  Pallas kernels  234 us (94%)
  local copies, waits for them, and re-layouts  13.6 us (5%)
    pallas_call x1, Pallas kernels, fused(): pl.pallas_call(functools.partial(fused_kernel, factor), out_shape=[jax.Sh...  234 us
    unnamed x16, local copies, waits for them, and re-layouts  13.6 us

profile of v4, /device:TPU:1, one launch (start us, length us, event | category | flops | bytes accessed | tf_op | source)
XLA Modules:
  0.0 247.8 jit_solution(5875243400705578864)
XLA Ops:
  0.6 233.6 %shard_map.163 = (bf16[1,512,2048]{2,1,0:T(8,128)(2,1)}, bf16[1,512,2048]{2,1,0:T(8,128)(2,1)}, bf16[1,512,2048]{2,1,0:T(8,128)(2,1)}, bf16[1,512,2048]{2,1,0:T(...) custom-call(bf16[1,512,2048]{2,1,0:T(8,128)(2,1)} %q_hbm.1, bf16[1,512,2048]{2,1,0:T(8,128)(2,1)} %k_hbm.1, ...), custom_call_target="tpu_custom_call" | custom-call | flops 44291850240 | bytes 25165824 | tf_op jit(solution)/shard_map/pallas_call | solution.py:525
  234.3 0.0 copy-start.3
  234.3 3.3 %copy.24 = bf16[1,512,2048]{2,1,0:T(8,128)(2,1)} copy(bf16[1,512,2048]{2,1,0:T(8,128)(2,1)} %get-tuple-element.24) | data formatting | bytes 4194304
  237.6 0.0 copy-done.3
  237.6 0.0 copy-start.2
  237.6 1.3 copy.25
  238.9 1.0 copy-done.2
  239.9 0.0 copy-start.1
  239.9 1.3 copy.26
  241.3 1.0 copy-done.1
  242.3 0.0 copy-start
  242.3 1.3 copy.27
  243.6 1.6 copy-done
  245.2 0.0 copy-start.4
  245.2 2.0 copy.28
  247.2 0.0 copy-done.4
  247.2 0.6 copy.29
Async XLA Ops:
  234.3 3.3 %copy-start.3 = (bf16[1,512,2048]{2,1,0:T(8,128)(2,1)S(1)}, bf16[1,512,2048]{2,1,0:T(8,128)(2,1)}, u32[]{:S(2)}) copy-start(bf16[1,512,2048]{2,1,0:T(8,128)(2,1)} %get-tuple-element.25) | copy-start | bytes 6291460
  237.6 2.3 copy-start.2
  239.9 2.3 copy-start.1
  242.3 2.9 %copy-start = (f32[512,2048]{1,0:T(8,128)S(1)}, f32[512,2048]{1,0:T(8,128)}, u32[]{:S(2)}) copy-start(f32[512,2048]{1,0:T(8,128)} %get-tuple-element.28) | copy-start | bytes 12582916
  245.2 2.0 copy-start.4

commit v5 on v4

--- a/solution.py
+++ b/solution.py
@@ -71,10 +71,10 @@
         return pl.ds(pl.multiple_of(blk * LANES, LANES), LANES)
 
     def upper_owner(k):
-        return jnp.where(jnp.logical_and(lax.rem(k, 2) == 1, k < 6), 3, 2)
+        return jnp.where(k == 1, 3, 2)
 
     def merge_order(m):
-        order = [0, 2, 4, 6, 1, 3, 5, 7] + list(range(8, steps))
+        order = [0, 2, 3, 4, 1] + list(range(5, steps))
         k = 0
         for i, step in enumerate(order):
             k = k + jnp.where(m == i, step, 0)
@@ -407,19 +407,26 @@
 
     @pl.when(z == 1)
     def _():
+        def pass_on(k):
+            for s in range(4):
+                arrived(xs.at[k, s], x_recv.at[k, s])
+            for s in range(2):
+                arrived(hs.at[k, s], h_recv.at[k, s])
+            forward_low(k, move)
+
+            @pl.when(k < steps - ahead)
+            def _():
+                give_across(k + ahead, move)
+
+        pass_on(0)
+
         def step(k, carry):
+            @pl.when(k < steps - 1)
+            def _():
+                pass_on(k + 1)
+
             @pl.when(k < steps)
             def _():
-                for s in range(4):
-                    arrived(xs.at[k, s], x_recv.at[k, s])
-                for s in range(2):
-                    arrived(hs.at[k, s], h_recv.at[k, s])
-                forward_low(k, move)
-
-                @pl.when(k < steps - ahead)
-                def _():
-                    give_across(k + ahead, move)
-
                 for s in range(4):
                     arrived(ws.at[k, s], w_recv.at[k, s])
                 transform(k, True)

time: 248 us -> 234 us (0.944)
  Pallas kernels: 234 us -> 219 us
    pallas_call x1, Pallas kernels: 234 us -> 219 us  [fused(): pl.pallas_call(functools.partial(fused_kernel, factor), out_shape=[jax.Sh...]
where the time goes in v5:
time: 234 us
  Pallas kernels  219 us (94%)
  local copies, waits for them, and re-layouts  13.6 us (6%)
    pallas_call x1, Pallas kernels, fused(): pl.pallas_call(functools.partial(fused_kernel, factor), out_shape=[jax.Sh...  219 us
    unnamed x16, local copies, waits for them, and re-layouts  13.6 us

profile of v5, /device:TPU:1, one launch (start us, length us, event | category | flops | bytes accessed | tf_op | source)
XLA Modules:
  0.0 233.6 jit_solution(16575489524878348728)
XLA Ops:
  0.6 219.4 %shard_map.163 = (bf16[1,512,2048]{2,1,0:T(8,128)(2,1)}, bf16[1,512,2048]{2,1,0:T(8,128)(2,1)}, bf16[1,512,2048]{2,1,0:T(8,128)(2,1)}, bf16[1,512,2048]{2,1,0:T(...) custom-call(bf16[1,512,2048]{2,1,0:T(8,128)(2,1)} %q_hbm.1, bf16[1,512,2048]{2,1,0:T(8,128)(2,1)} %k_hbm.1, ...), custom_call_target="tpu_custom_call" | custom-call | flops 44291850240 | bytes 25165824 | tf_op jit(solution)/shard_map/pallas_call | solution.py:532
  220.0 0.0 copy-start.3
  220.0 3.3 %copy.24 = bf16[1,512,2048]{2,1,0:T(8,128)(2,1)} copy(bf16[1,512,2048]{2,1,0:T(8,128)(2,1)} %get-tuple-element.24) | data formatting | bytes 4194304
  223.3 0.0 copy-done.3
  223.3 0.0 copy-start.2
  223.3 1.3 copy.25
  224.6 1.0 copy-done.2
  225.7 0.0 copy-start.1
  225.7 1.3 copy.26
  227.0 1.0 copy-done.1
  228.0 0.0 copy-start
  228.0 1.3 copy.27
  229.3 1.6 copy-done
  231.0 0.0 copy-start.4
  231.0 2.0 copy.28
  233.0 0.0 copy-done.4
  233.0 0.6 copy.29
Async XLA Ops:
  220.0 3.3 %copy-start.3 = (bf16[1,512,2048]{2,1,0:T(8,128)(2,1)S(1)}, bf16[1,512,2048]{2,1,0:T(8,128)(2,1)}, u32[]{:S(2)}) copy-start(bf16[1,512,2048]{2,1,0:T(8,128)(2,1)} %get-tuple-element.25) | copy-start | bytes 6291460
  223.3 2.3 %copy-start.2 = (bf16[1,512,2048]{2,1,0:T(8,128)(2,1)S(1)}, bf16[1,512,2048]{2,1,0:T(8,128)(2,1)}, u32[]{:S(2)}) copy-start(bf16[1,512,2048]{2,1,0:T(8,128)(2,1)} %get-tuple-element.26) | copy-start | bytes 6291460
  225.7 2.3 %copy-start.1 = (bf16[1,512,2048]{2,1,0:T(8,128)(2,1)S(1)}, bf16[1,512,2048]{2,1,0:T(8,128)(2,1)}, u32[]{:S(2)}) copy-start(bf16[1,512,2048]{2,1,0:T(8,128)(2,1)} %get-tuple-element.27) | copy-start | bytes 6291460
  228.0 2.9 %copy-start = (f32[512,2048]{1,0:T(8,128)S(1)}, f32[512,2048]{1,0:T(8,128)}, u32[]{:S(2)}) copy-start(f32[512,2048]{1,0:T(8,128)} %get-tuple-element.28) | copy-start | bytes 12582916
  231.0 2.0 copy-start.4
